TPU v7x, 512 devices: a whole 4x4x16 slice. The times are simulated.
512 devices in a mesh: row: 16 (over x, y_hi, core), col: 32 (over y_lo, z).
Axes of the slice: x: 4, y: 4 (y_hi: 2, y_lo: 2; y = y_hi * 2 + y_lo), z: 16, core: 2. Of those that a mesh axis runs over, the one named last changes fastest.
Arguments:
- pair: bfloat16 [640, 640, 128], P('row', 'col'), may hold values from -6 to 6
- norm_gain: float32 [128], replicated, may hold values from 0.1 to 1.9
- proj_weight: bfloat16 [128, 512], replicated, may hold values from -0.5 to 0.5
- gate_weight: bfloat16 [128, 128], replicated, may hold values from -0.5 to 0.5
- out_gain: float32 [128], replicated, may hold values from 0.1 to 1.9
- out_weight: bfloat16 [128, 128], replicated, may hold values from -0.5 to 0.5
Outputs:
- updated: bfloat16 [640, 640, 128], P('row', 'col')
All inputs are finite; a program needn't handle non-finite values.
Results may differ from a plain program's by a relative error of at most 0.0054.
Values may be sent and summed in bfloat16 or wider, within the bound.
A program may use at most 128 MiB of HBM per device.

v0:
```python
import jax
import jax.numpy as jnp
from jax import lax
from jax.sharding import PartitionSpec as P

epsilon = 1e-05


def layer_norm(values, weights):
    center = jnp.mean(values, axis=-1, keepdims=True)
    shifted = values - center
    spread = jnp.mean(shifted * shifted, axis=-1, keepdims=True)
    return shifted * lax.rsqrt(spread + epsilon) * weights


def shards(pair, norm_gain, proj_weight, gate_weight, out_gain, out_weight):
    row_count, col_count, channels = pair.shape
    hidden = out_weight.shape[0]
    widened = pair.astype(jnp.float32)
    normed = layer_norm(widened, norm_gain).astype(jnp.bfloat16)
    flat_normed = normed.reshape(row_count * col_count, channels)
    projected = jnp.dot(flat_normed, proj_weight, preferred_element_type=jnp.float32).reshape(
        row_count, col_count, 4 * hidden
    )
    left_factor = (
        jax.nn.sigmoid(projected[..., 0:hidden]) * projected[..., hidden : 2 * hidden]
    ).astype(jnp.bfloat16)
    right_factor = (
        jax.nn.sigmoid(projected[..., 2 * hidden : 3 * hidden]) * projected[..., 3 * hidden :]
    ).astype(jnp.bfloat16)
    left_major = jnp.transpose(left_factor, (2, 0, 1))
    right_major = jnp.transpose(right_factor, (2, 0, 1))
    gating = jax.nn.sigmoid(
        jnp.dot(flat_normed, gate_weight, preferred_element_type=jnp.float32)
    ).reshape(row_count, col_count, channels)
    right_all = lax.all_gather(right_major, "row", axis=1, tiled=True)
    right_rows = lax.all_to_all(right_all, "col", split_axis=1, concat_axis=2, tiled=True)
    summed_major = jnp.einsum(
        "cik,cjk->cij",
        lax.all_gather(left_major, "col", axis=2, tiled=True),
        right_rows,
        preferred_element_type=jnp.float32,
    )
    summed = jnp.transpose(summed_major, (1, 2, 0))
    mixed_low = layer_norm(summed, out_gain).astype(jnp.bfloat16)
    update = jnp.dot(
        mixed_low.reshape(row_count * col_count, hidden),
        out_weight,
        preferred_element_type=jnp.float32,
    ).reshape(row_count, col_count, channels)
    return (widened + gating * update).astype(jnp.bfloat16)


def solution(mesh):
    in_specs = (P("row", "col", None), P(), P(), P(), P(), P())
    out_specs = P("row", "col", None)
    return jax.shard_map(shards, mesh=mesh, in_specs=in_specs, out_specs=out_specs, check_vma=False)
```

profile of v0, /device:TPU:2, one launch (start us, length us, event | category | flops | bytes accessed | tf_op | source)
XLA Modules:
  0.0 432.4 jit_solution(4235047988753577560)
XLA Ops:
  6.5 0.0 copy-start
  6.5 0.0 all-gather.5.cloned.1.call-start
  6.5 1.1 convert_reduce_fusion
  7.7 1.3 fusion.8
  9.0 1.2 fusion.10
  10.2 0.4 fusion.21
  10.6 1.0 fusion.20
  11.5 0.0 all-gather.5.cloned.1.call-update
  11.6 0.0 all-gather.3.cloned.1.call-start
  11.6 0.7 all-gather.3.cloned.1.call-update
  12.3 71.6 %all-gather.5.cloned.1.call-done = bf16[128,640,20]{0,1,2:T(8,128)(2,1)} async-done(((bf16[128,40,20]{0,1,2:T(8,128)(2,1)}), bf16[128,640,20]{0,1,2:T(8,128)(2,1)}) %all-gather.5.cloned.1.call-update) | async-done | bytes 3276816 | tf_op jit(solution)/shard_map/all_gather | solution.py:36
  83.9 6.0 %copy.18 = bf16[128,640,20]{0,2,1:T(8,128)(2,1)} copy(bf16[128,640,20]{0,1,2:T(8,128)(2,1)} %all-gather.5.cloned.1.call-done) | data formatting | bytes 6553600 | tf_op jit(solution)/shard_map/all_gather | solution.py:36
  89.9 12.8 %all-to-all-start = ((bf16[128,640,20]{0,2,1:T(8,128)(2,1)}), bf16[128,640,20]{0,2,1:T(8,128)(2,1)}, u32[]{:S(2)}, u32[]{:S(2)}) async-start(bf16[128,640,20]{0,2,1:T(8,128)(2,1)} %copy.18), calls=%async_computation | async-start | bytes 7864320 | tf_op jit(solution)/shard_map/all_to_all | solution.py:37
  102.9 0.3 fusion.2
  103.1 0.8 reshape.40
  103.9 267.1 %all-gather.3.cloned.1.call-done = bf16[128,40,640]{0,1,2:T(8,128)(2,1)} async-done(((bf16[128,40,20]{0,1,2:T(8,128)(2,1)}), bf16[128,40,640]{0,1,2:T(8,128)(2,1)}) %all-gather.3.cloned.1.call-update) | async-done | bytes 6553616 | tf_op jit(solution)/shard_map/all_gather | solution.py:40
  371.1 28.6 %copy.21 = bf16[128,40,640]{1,2,0:T(8,128)(2,1)} copy(bf16[128,40,640]{0,1,2:T(8,128)(2,1)} %all-gather.3.cloned.1.call-done) | data formatting | bytes 13107200 | tf_op jit(solution)/shard_map/all_gather | solution.py:40
  399.7 0.0 all-to-all-done
  399.7 5.0 %copy.20 = bf16[128,20,32,20]{0,3,2,1:T(8,128)(2,1)} copy(bf16[128,20,32,20]{0,3,1,2:T(8,128)(2,1)} %bitcast.5) | data formatting | bytes 6553600 | tf_op jit(solution)/shard_map/all_to_all | solution.py:37
  404.8 4.7 %all_to_all.16 = bf16[128,20,640]{0,2,1:T(8,128)(2,1)S(1)} reshape(bf16[128,20,32,20]{0,3,2,1:T(8,128)(2,1)} %copy.20) | data formatting | bytes 6553600 | tf_op jit(solution)/shard_map/all_to_all | solution.py:37
  409.5 4.1 copy.22
  413.5 9.8 %bitcast_reduce_fusion = (f32[40,20]{0,1:T(8,128)S(1)}, f32[128,40,20]{1,2,0:T(8,128)S(1)}) fusion(bf16[128,40,640]{1,2,0:T(8,128)(2,1)} %copy.21, bf16[128,20,640]{2,1,0:T(8,128)(2,1)} %copy.22), kind=kOutput, calls=%fused_computation.1 | convolution fusion | flops 131173600 | bytes 10243200 | tf_op jit(solution)/shard_map/cik,cjk->cij/dot_general | solution.py:38
  423.4 0.0 copy-start.4
  423.4 0.0 copy-start.1
  423.4 0.0 copy-start.3
  423.5 0.3 multiply_reduce_fusion
  423.7 0.3 copy-done.4
  424.1 0.3 multiply_convert_fusion
  424.3 0.0 copy-done.1
  424.4 0.2 copy-done.2
  424.6 0.0 copy-done.3
  424.6 1.0 fusion.4
  (10 shorter events, 0.1 us)
Async XLA Ops:
  6.5 3.7 copy-start
  6.5 77.4 %all-gather.5.cloned.1.call-start = ((), (), s32[]{:S(2)}) async-start(), calls=%async_computation.2 | async-start | bytes 3481600 | tf_op jit(solution)/shard_map/all_gather | solution.py:36
  11.6 359.5 %all-gather.3.cloned.1.call-start = ((), (), s32[]{:S(2)}) async-start(), calls=%async_computation.1 | async-start | bytes 6758400 | tf_op jit(solution)/shard_map/all_gather | solution.py:40
  89.9 13.0 %copy-start.5 = (bf16[128,128]{1,0:T(8,128)(2,1)S(1)}, bf16[128,128]{1,0:T(8,128)(2,1)}, u32[]{:S(2)}) copy-start(bf16[128,128]{1,0:T(8,128)(2,1)} %param.9) | copy-start | bytes 98308
  89.9 309.8 %all-to-all-start = ((bf16[128,640,20]{0,2,1:T(8,128)(2,1)}), bf16[128,640,20]{0,2,1:T(8,128)(2,1)}, u32[]{:S(2)}, u32[]{:S(2)}) async-start(bf16[128,640,20]{0,2,1:T(8,128)(2,1)} %copy.18), calls=%async_computation | async-start | bytes 7864320 | tf_op jit(solution)/shard_map/all_to_all | solution.py:37
  423.4 0.7 copy-start.4
  423.4 0.9 copy-start.1
  423.4 1.1 copy-start.2
  423.4 1.1 copy-start.3
Sparse Core Ops, SparseCore 0:
  11.7 72.2 all-gather.4
  86.0 285.0 all-gather.2
where the time goes:
time: 433 us; the launch traced here: 432 us
  waiting for transfers between devices  339 us (78%)
  local copies, waits for them, and re-layouts  49.9 us (12%)
  between operations  13.5 us (3%)
  starting transfers between devices  12.9 us (3%)
  matrix products  11.5 us (3%)
  other arithmetic  5.12 us (1%)
    all_gather x1, waiting for transfers between devices, shards(): lax.all_gather(left_major, 'col', axis=2, tiled=True)  267 us
    all_gather x1, waiting for transfers between devices, shards(): right_all = lax.all_gather(right_major, 'row', axis=1, tiled=True)  71.6 us
    all_gather x1, local copies, waits for them, and re-layouts, shards(): lax.all_gather(left_major, 'col', axis=2, tiled=True)  28.6 us
    all_to_all x3, local copies, waits for them, and re-layouts, shards(): lax.all_to_all(right_all, 'col', split_axis=1, concat_axis=2, tiled=True)  13.8 us
    all_to_all x1, starting transfers between devices, shards(): lax.all_to_all(right_all, 'col', split_axis=1, concat_axis=2, tiled=True)  12.8 us
    dot_general x1, matrix products, shards(): jnp.einsum('cik,cjk->cij', lax.all_gather(left_major, 'col', axis=2, tile...  9.84 us
  transfers between devices with their start and end apart: 3, of which 2 were waited for; matrix products, arithmetic and copies ran while one was open for 8% of the time, Pallas kernels for 0%

commit v1 on v0

v1 whole, which is shorter than its diff:
```python
import jax
import jax.numpy as jnp
from jax import lax
from jax.experimental import pallas as pl
from jax.experimental.pallas import tpu as pltpu
from jax.sharding import PartitionSpec as P

MESH = pl.DeviceIdType.MESH
F32 = jnp.float32
BF16 = jnp.bfloat16
EPS = 1e-05
NZ = 16
ROWS = 40
COLS = 20
PITCH = 24
NG = 7
CHUNKS = ((0, 2), (2, 2), (4, 2), (6, 1))
NCH = len(CHUNKS)
KROWS = 2 * 3 * NG * NZ


def lanes_of(shape):
    return lax.broadcasted_iota(jnp.int32, shape, 1)


def rows_of(shape):
    return lax.broadcasted_iota(jnp.int32, shape, 0)


def kernel(pair_ref, ngain_ref, proj_ref, gatew_ref, ogain_ref, outw_ref, out_ref,
           pf, nf, gat, wt, zs, zr, tb, ps, lb, rb, lt, rt_, st, tiles, sib, comb, back, xn, gcol, wf,
           zss, zrs, lss, lrs, rss, rrs, ess, ers, bss, brs):
    row = lax.axis_index("row")
    col = lax.axis_index("col")
    z, yl = col % NZ, col // NZ
    x1, x0, yh, core = row // 8, (row // 4) % 2, (row // 2) % 2, row % 2

    def dev(ax1, ax0, ayh, acore, ayl, az):
        return {"row": ax1 * 8 + ax0 * 4 + ayh * 2 + acore, "col": ayl * NZ + az}

    def left_target(n):
        return (x1, (x0 + n // 8) % 2, (yh + (n // 4) % 2) % 2, (core + (n // 2) % 2) % 2, (yl + n % 2) % 2)

    def right_target(n):
        return ((x1 + n // 8) % 2, (x0 + (n // 4) % 2) % 2, yh, (core + (n // 2) % 2) % 2, (yl + n % 2) % 2)

    barrier = pltpu.get_barrier_semaphore()

    def greet(t, az):
        pl.semaphore_signal(barrier, inc=1, device_id=dev(*t, az), device_id_type=MESH)

    @pl.loop(1, NZ)
    def _(d):
        greet((x1, x0, yh, core, yl), (z + d) % NZ)

    @pl.loop(1, 16)
    def _(n):
        greet(left_target(n), z)

    @pl.loop(8, 16)
    def _(n):
        greet(right_target(n), z)

    @pl.loop(0, ROWS)
    def _(i):
        base = pl.multiple_of(i * PITCH, 8)
        pf[pl.ds(base + 16, 8), :] = jnp.zeros((8, 128), F32)
        pf[pl.ds(base, COLS), :] = pair_ref[i].astype(F32)

    wt[...] = proj_ref[...].astype(F32).T.astype(BF16)
    ngain = ngain_ref[...]

    for g in range(NG):
        for s in range(3):
            v = pf[pl.ds(3 * g + s, ROWS, stride=PITCH), :]
            center = jnp.mean(v, axis=-1, keepdims=True)
            shifted = v - center
            spread = jnp.mean(shifted * shifted, axis=-1, keepdims=True)
            nf[128 * g + 40 * s : 128 * g + 40 * s + 40, :] = shifted * lax.rsqrt(spread + EPS) * ngain
        nf[128 * g + 120 : 128 * g + 128, :] = jnp.zeros((8, 128), F32)

    nt = (((1,), (1,)), ((), ()))

    @pl.loop(0, NG)
    def _(g):
        n_g = nf[pl.ds(pl.multiple_of(g * 128, 128), 128), :].astype(BF16)
        p = lax.dot_general(wt[...], n_g, nt, preferred_element_type=F32)
        left = jax.nn.sigmoid(p[0:128]) * p[128:256]
        right = jax.nn.sigmoid(p[256:384]) * p[384:512]
        for t in range(NZ):
            zs[t, g] = jnp.concatenate([left[8 * t : 8 * t + 8], right[8 * t : 8 * t + 8]], axis=0).astype(BF16)

    pl.semaphore_wait(barrier, 15 + 15 + 8)

    def z_copy(ci, d):
        g0, n = CHUNKS[ci]
        t = (z + d) % NZ
        return pltpu.make_async_remote_copy(
            src_ref=zs.at[t, pl.ds(g0, n)], dst_ref=zr.at[z, pl.ds(g0, n)],
            send_sem=zss.at[ci, d], recv_sem=zrs.at[ci, d],
            device_id=dev(x1, x0, yh, core, yl, t), device_id_type=MESH)

    for ci in range(NCH):
        @pl.loop(0, 15)
        def _(k, ci=ci):
            d = 8 + (k + 1) // 2 * (1 - 2 * (k % 2))
            z_copy(ci, d).start()

    zr[z] = zs[z]

    @pl.loop(0, NG)
    def _(g):
        rows = pl.ds(pl.multiple_of(g * 128, 128), 128)
        gat[rows, :] = jax.nn.sigmoid(jnp.dot(nf[rows, :].astype(BF16), gatew_ref[...], preferred_element_type=F32))

    gcol[...] = jnp.broadcast_to(ogain_ref[...], (128, 128)).T
    wf[...] = outw_ref[...].astype(F32)

    def l_copy(ci, n):
        g0, m = CHUNKS[ci]
        t = left_target(n)
        return pltpu.make_async_remote_copy(
            src_ref=ps.at[t[1] * 4 + t[4] * 2 + t[3], pl.ds(g0, m)],
            dst_ref=lb.at[(x0 * 4 + yh * 2 + core) * 2 + yl, pl.ds(g0, m)],
            send_sem=lss.at[ci, n], recv_sem=lrs.at[ci, n], device_id=dev(*t, z), device_id_type=MESH)

    def r_copy(ci, n):
        g0, m = CHUNKS[ci]
        t = right_target(n)
        return pltpu.make_async_remote_copy(
            src_ref=ps.at[8 + t[1] * 4 + t[4] * 2 + t[3], pl.ds(g0, m)],
            dst_ref=rb.at[(x1 * 4 + x0 * 2 + core) * 2 + yl, pl.ds(g0, m)],
            send_sem=rss.at[ci, n], recv_sem=rrs.at[ci, n], device_id=dev(*t, z), device_id_type=MESH)

    channel = x0 * 4 + yl * 2 + core
    lane = lanes_of((NZ, 128))

    def regroup(src, dst, g):
        for y in range(2):
            for q in range(3):
                parts = [src[(3 * q + s) * 2 + y, g].astype(F32) for s in range(3 if q < 2 else 2)]
                for k in range(3):
                    moved = [pltpu.roll(v, (40 * (s - k)) % 128, 1) if s != k else v for s, v in enumerate(parts)]
                    tile = jnp.where(lane < 40, moved[0], moved[1])
                    if len(moved) > 2:
                        tile = jnp.where(lane < 80, tile, moved[2])
                    dst[pl.ds(pl.multiple_of(((y * NG + g) * 3 + k) * NZ, NZ), NZ), q * 128 : q * 128 + 128] = tile.astype(BF16)

    def plane_in(ci):
        g0, m = CHUNKS[ci]

        @pl.loop(1, 16)
        def _(n):
            l_copy(ci, n).wait_recv()
            r_copy(ci, n).wait_recv()

        @pl.loop(g0, g0 + m)
        def _(g):
            regroup(lb, lt, g)
            regroup(rb, rt_, g)

    for ci in range(NCH):
        g0, m = CHUNKS[ci]

        @pl.loop(1, NZ)
        def _(d, ci=ci):
            z_copy(ci, d).wait_recv()

        @pl.loop(g0, g0 + m)
        def _(g):
            for t in range(NZ):
                tb[16 * t : 16 * t + 16, :] = zr[t, g].astype(F32)
            for c in range(16):
                ps[c, g] = tb[pl.ds(c, NZ, stride=16), :].astype(BF16)

        @pl.loop(1, 16)
        def _(n, ci=ci):
            l_copy(ci, n).start()
            r_copy(ci, n).start()

        lb[(x0 * 4 + yh * 2 + core) * 2 + yl, pl.ds(g0, m)] = ps[channel, pl.ds(g0, m)]
        rb[(x1 * 4 + x0 * 2 + core) * 2 + yl, pl.ds(g0, m)] = ps[8 + channel, pl.ds(g0, m)]
        if ci > 0:
            plane_in(ci - 1)
    plane_in(NCH - 1)

    tn = (((0,), (0,)), ((), ()))
    st[...] = lax.dot_general(rt_[...], lt[...], tn, preferred_element_type=F32)

    for half in range(2):
        mine = half == core
        shift = jnp.where(mine, 0, 40)
        main = (lane >= shift) & (lane < shift + 40)
        erow = jnp.where(mine, 0, 8)
        rowi = rows_of((NZ, 128))
        extra = (lane >= 80) & (lane < 120) & (rowi >= erow) & (rowi < erow + 4)
        for jj in range(4):
            rj = 4 * half + jj
            for h in range(2):
                base = 128 * (rj // 3) + 40 * (rj % 3) + 20 * h
                for q in range(3):
                    a = st[base : base + 16, 128 * q : 128 * q + 128]
                    b = st[base + 16 : base + 24, 128 * q : 128 * q + 128]
                    b = jnp.concatenate([b, b], axis=0)
                    for s in range(3 if q < 2 else 2):
                        am = pltpu.roll(a, (shift - 40 * s + 128) % 128, 1)
                        bm = pltpu.roll(b, (80 - 40 * s) % 128, 1) if s != 2 else b
                        tile = jnp.where(main, am, jnp.where(extra, bm, 0.0))
                        tiles[half, (jj * 2 + h) * 8 + 3 * q + s] = tile.astype(BF16)

    swap = pltpu.make_async_remote_copy(
        src_ref=tiles.at[1 - core], dst_ref=sib, send_sem=ess, recv_sem=ers,
        device_id=dev(x1, x0, yh, 1 - core, yl, z), device_id_type=MESH)
    swap.start()
    swap.wait_recv()

    m_me = z * 4 + x0 * 2 + yl

    def b_target(n):
        j = (n // 8 + z) % 8
        i = (n + x0 * 4 + yh * 2 + core) % 8
        zt = 8 * (j // 4) + 4 * yh + 2 * ((j // 2) % 2) + j % 2
        same = (i == x0 * 4 + yh * 2 + core) & (core == yl) & (zt == z)
        return j * 8 + i, dev(x1, i // 4, (i // 2) % 2, i % 2, core, zt), same

    def b_copy(n):
        k, d, same = b_target(n)
        return same, k, pltpu.make_async_remote_copy(
            src_ref=comb.at[k], dst_ref=back.at[m_me], send_sem=bss, recv_sem=brs, device_id=d, device_id_type=MESH)

    @pl.loop(0, 64)
    def _(n):
        same, k, cp = b_copy(n)
        comb[k] = (tiles[core, k].astype(F32) + sib[k].astype(F32)).astype(BF16)

        @pl.when(jnp.logical_not(same))
        def _():
            cp.start()

        @pl.when(same)
        def _():
            pltpu.make_async_copy(comb.at[k], back.at[m_me], brs).start()

    pltpu.make_async_copy(comb, back, brs).wait()

    def total(step):
        def add(m, acc):
            for u in range(8):
                acc = acc + step(m * 8 + u)
            return acc
        s = lax.fori_loop(0, 8, add, jnp.zeros((NZ, 128), F32))
        both = s + pltpu.roll(s, 88, 1)
        e = s[0:8] + s[8:16]
        return jnp.where(lane < 40, both, jnp.where(lane < 80, pltpu.roll(both, 40, 1), jnp.concatenate([e, e], axis=0))) * (1.0 / 128.0)

    mean = total(lambda m: back[m].astype(F32))

    def square(m):
        d = back[m].astype(F32) - mean
        return d * d
    scale = lax.rsqrt(total(square) + EPS)

    @pl.loop(0, 64)
    def _(m):
        xn[pl.ds(pl.multiple_of(m * 16, 16), 16), :] = (back[m].astype(F32) - mean) * scale

    even, odd = gcol[pl.ds(0, 64, stride=2), :], gcol[pl.ds(1, 64, stride=2), :]
    g_a, g_b = jnp.where(yl == 0, even, odd), jnp.where(yl == 0, odd, even)
    even, odd = wf[pl.ds(0, 64, stride=2), :], wf[pl.ds(1, 64, stride=2), :]
    w_ab = jnp.concatenate([jnp.where(yl == 0, even, odd), jnp.where(yl == 0, odd, even)], axis=1).astype(BF16)
    lane64 = lanes_of((64, 128))
    rest = {}
    for t in range(16):
        gain = jnp.where(lane64 < 40, g_a, jnp.where(lane64 < 80, g_b, g_a if t < 8 else g_b))
        x = (xn[pl.ds(t, 64, stride=16), :] * gain).astype(BF16)
        y = lax.dot_general(x, w_ab, tn, preferred_element_type=F32)
        done = [(t, y[0:40, 0:128] + y[40:80, 128:256])]
        if t < 4:
            rest[t] = y[80:120, 0:128]
        if 8 <= t < 12:
            done.append((t + 8, rest[t - 8] + y[80:120, 128:256]))
        for k, u in done:
            at = 128 * (k // 3) + 40 * (k % 3)
            pf[pl.ds(k, ROWS, stride=PITCH), :] = pf[pl.ds(k, ROWS, stride=PITCH), :] + gat[at : at + 40, :] * u

    @pl.loop(0, ROWS)
    def _(i):
        out_ref[i] = pf[pl.ds(pl.multiple_of(i * PITCH, 8), COLS), :].astype(BF16)

    for ci in range(NCH):
        @pl.loop(1, 16)
        def _(n, ci=ci):
            z_copy(ci, n).wait_send()
            l_copy(ci, n).wait_send()
            r_copy(ci, n).wait_send()
    swap.wait_send()

    @pl.loop(0, 64)
    def _(n):
        same, k, cp = b_copy(n)

        @pl.when(jnp.logical_not(same))
        def _():
            cp.wait_send()


def shards(pair, norm_gain, proj_weight, gate_weight, out_gain, out_weight):
    vm = pl.BlockSpec(memory_space=pltpu.VMEM)
    dma = pltpu.SemaphoreType.DMA
    return pl.pallas_call(
        kernel,
        out_shape=jax.ShapeDtypeStruct(pair.shape, BF16),
        in_specs=[vm] * 6,
        out_specs=vm,
        scratch_shapes=[
            pltpu.VMEM((ROWS * PITCH, 128), F32),
            pltpu.VMEM((NG * 128, 128), F32),
            pltpu.VMEM((NG * 128, 128), F32),
            pltpu.VMEM((512, 128), BF16),
            pltpu.VMEM((NZ, NG, 16, 128), BF16),
            pltpu.VMEM((NZ, NG, 16, 128), BF16),
            pltpu.VMEM((256, 128), F32),
            pltpu.VMEM((16, NG, 16, 128), BF16),
            pltpu.VMEM((16, NG, 16, 128), BF16),
            pltpu.VMEM((16, NG, 16, 128), BF16),
            pltpu.VMEM((KROWS, 384), BF16),
            pltpu.VMEM((KROWS, 384), BF16),
            pltpu.VMEM((384, 384), F32),
            pltpu.VMEM((2, 64, 16, 128), BF16),
            pltpu.VMEM((64, 16, 128), BF16),
            pltpu.VMEM((64, 16, 128), BF16),
            pltpu.VMEM((64, 16, 128), BF16),
            pltpu.VMEM((1024, 128), F32),
            pltpu.VMEM((128, 128), F32),
            pltpu.VMEM((128, 128), F32),
            dma((NCH, 16)), dma((NCH, 16)),
            dma((NCH, 16)), dma((NCH, 16)),
            dma((NCH, 16)), dma((NCH, 16)),
            dma, dma, dma, dma,
        ],
        compiler_params=pltpu.CompilerParams(collective_id=0, has_side_effects=True, vmem_limit_bytes=40 * 1024 * 1024),
        name="triangle",
    )(pair, norm_gain.reshape(1, -1), proj_weight, gate_weight, out_gain.reshape(1, -1), out_weight)


def solution(mesh):
    in_specs = (P("row", "col", None), P(), P(), P(), P(), P())
    return jax.shard_map(shards, mesh=mesh, in_specs=in_specs, out_specs=P("row", "col", None), check_vma=False)
```

time: 433 us -> 77.6 us (0.18)
  the two profiles are of different devices: /device:TPU:2 before, /device:TPU:1 now
where the time goes in v1:
time: 77.6 us; the launch traced here: 77.5 us
  Pallas kernels  75.7 us (98%)
  local copies, waits for them, and re-layouts  1.74 us (2%)
    pallas_call x1, Pallas kernels, shards(): pl.pallas_call(kernel, out_shape=jax.ShapeDtypeStruct(pair.shape, BF16),...  75.7 us

profile of v1, /device:TPU:1, one launch (start us, length us, event | category | flops | bytes accessed | tf_op | source)
XLA Modules:
  0.0 77.5 jit_solution(3260755268543642573)
XLA Ops:
  0.0 0.0 copy-start
  0.0 0.0 copy-start.1
  0.0 0.0 copy-start.2
  0.0 0.0 copy-start.3
  0.0 0.0 copy-start.4
  0.0 1.0 %copy.7.pair_ref = bf16[40,20,128]{2,1,0:T(8,128)(2,1)S(1)} copy(bf16[40,20,128]{2,0,1:T(8,128)(2,1)} %param.6) | data formatting | bytes 409600 | tf_op args[0]
  1.0 0.0 copy-done
  1.1 0.0 copy-done.1
  1.1 0.0 copy-done.2
  1.1 0.0 copy-done.3
  1.1 0.0 copy-done.4
  1.1 75.7 %triangle.1 = bf16[40,20,128]{2,1,0:T(8,128)(2,1)S(1)} custom-call(bf16[40,20,128]{2,1,0:T(8,128)(2,1)S(1)} %copy.7.pair_ref, f32[1,128]{1,0:T(1,128)S(1)} %bitcast.2, bf16[128,512]{1,0:T(8,128)(2,1)S(1)} %copy-done, bf16[128,128]{1,0:T(8,128)(2,1)S(1)} %copy-done.1, f32[1,128]{1,0:T(1,128)S(1)} %bitcast.3, bf16[128,128]{1,0:T(8,128)(2,1)S(1)} %copy-done.2), custom_call_target="tpu_custom_call" | custom-call | tf_op jit(solution)/shard_map/triangle/pallas_call | solution.py:310
  76.8 0.7 copy.8
Async XLA Ops:
  0.0 1.0 %copy-start = (bf16[128,512]{1,0:T(8,128)(2,1)S(1)}, bf16[128,512]{1,0:T(8,128)(2,1)}, u32[]{:S(2)}) copy-start(bf16[128,512]{1,0:T(8,128)(2,1)} %proj_ref.1) | copy-start | bytes 393220
  0.0 1.1 %copy-start.1 = (bf16[128,128]{1,0:T(8,128)(2,1)S(1)}, bf16[128,128]{1,0:T(8,128)(2,1)}, u32[]{:S(2)}) copy-start(bf16[128,128]{1,0:T(8,128)(2,1)} %gatew_ref.1) | copy-start | bytes 98308
  0.0 1.1 %copy-start.2 = (bf16[128,128]{1,0:T(8,128)(2,1)S(1)}, bf16[128,128]{1,0:T(8,128)(2,1)}, u32[]{:S(2)}) copy-start(bf16[128,128]{1,0:T(8,128)(2,1)} %outw_ref.1) | copy-start | bytes 98308
  0.0 1.1 %copy-start.3 = (f32[128]{0:T(128)S(1)}, f32[128]{0:T(128)}, u32[]{:S(2)}) copy-start(f32[128]{0:T(128)} %param.7) | copy-start | bytes 1540
  0.0 1.1 %copy-start.4 = (f32[128]{0:T(128)S(1)}, f32[128]{0:T(128)}, u32[]{:S(2)}) copy-start(f32[128]{0:T(128)} %param.10) | copy-start | bytes 1540

commit v2 on v0

v2 whole, which is shorter than its diff:
```python
import jax
import jax.numpy as jnp
from jax import lax
from jax.experimental import pallas as pl
from jax.experimental.pallas import tpu as pltpu
from jax.sharding import PartitionSpec as P

MESH = pl.DeviceIdType.MESH
F32 = jnp.float32
BF16 = jnp.bfloat16
EPS = 1e-05
NZ = 16
ROWS = 40
COLS = 20
NG = 7
CHUNKS = ((0, 4), (4, 3))
NCH = len(CHUNKS)
KROWS = 2 * 3 * NG * NZ
NL = 4
BACK = ((0, 1), (1, 3))
NBC = len(BACK)


def lanes_of(shape):
    return lax.broadcasted_iota(jnp.int32, shape, 1)


def rows_of(shape):
    return lax.broadcasted_iota(jnp.int32, shape, 0)


def kernel(pair_in, ngain_in, proj_in, gatew_in, ogain_in, outw_in, out_ref,
           pair_ref, ngain_ref, proj_ref, gatew_ref, ogain_ref, outw_ref, nf, gat, wt, zs, zr, tb, ps, lb, rb, lt, rt_, total, st, tiles, back, zb, zo, gcol,
           zss, zrs, lss, lrs, rss, rrs, ess, ers, bss, brs, ins):
    row = lax.axis_index("row")
    col = lax.axis_index("col")
    z, yl = col % NZ, col // NZ
    x1, x0, yh, core = row // 8, (row // 4) % 2, (row // 2) % 2, row % 2

    flips = {"x1": (8 * (1 - 2 * x1), 0, 0), "x0": (4 * (1 - 2 * x0), 0, 4 * (1 - 2 * x0)), "yh": (2 * (1 - 2 * yh), 0, 0),
             "core": (1 - 2 * core, 0, 1 - 2 * core), "yl": (0, NZ * (1 - 2 * yl), 2 * (1 - 2 * yl))}
    channel = x0 * 4 + yl * 2 + core

    def flipped(names):
        r, c, k = row, col, channel
        for name in names:
            r, c, k = r + flips[name][0], c + flips[name][1], k + flips[name][2]
        return {"row": r, "col": c}, k

    def subsets(names):
        found = [[n for i, n in enumerate(names) if m >> i & 1] for m in range(1, 16)]
        return sorted(found, key=lambda f: -len(f))

    left_partners = subsets(("x0", "yh", "yl", "core"))
    right_partners = subsets(("x1", "x0", "yl", "core"))
    far_first = [8] + [d for k in range(7, 0, -1) for d in (k, NZ - k)]

    def along(d):
        t = lax.rem(z + d, NZ)
        return t, {"row": row, "col": yl * NZ + t}

    def remote(src, dst, send_sem, recv_sem, to):
        pltpu.make_async_remote_copy(
            src_ref=src, dst_ref=dst, send_sem=send_sem, recv_sem=recv_sem, device_id=to, device_id_type=MESH).start()

    def all_of(ref, sem):
        pltpu.make_async_copy(ref, ref, sem).wait()

    ins_from = (pair_in, proj_in, ngain_in, gatew_in, ogain_in, outw_in)
    ins_to = (pair_ref, proj_ref, ngain_ref, gatew_ref, ogain_ref, outw_ref)
    fetch = [pltpu.make_async_copy(a, b, ins.at[n]) for n, (a, b) in enumerate(zip(ins_from, ins_to))]
    for f in fetch:
        f.start()

    barrier = pltpu.get_barrier_semaphore()
    greeted = [along(d)[1] for d in far_first]
    greeted += [flipped(f)[0] for f in left_partners] + [flipped(f)[0] for f in right_partners if "x1" in f]
    for to in greeted:
        pl.semaphore_signal(barrier, inc=1, device_id=to, device_id_type=MESH)

    for f in fetch:
        f.wait()
    wt[...] = proj_ref[...].astype(F32).T.astype(BF16)
    ngain = ngain_ref[...]

    for g in range(NG):
        for s in range(3):
            at = 128 * g + 40 * s
            if 3 * g + s < COLS:
                v = pair_ref[3 * g + s].astype(F32)
                center = jnp.mean(v, axis=-1, keepdims=True)
                shifted = v - center
                spread = jnp.mean(shifted * shifted, axis=-1, keepdims=True)
                nf[at : at + 40, :] = shifted * lax.rsqrt(spread + EPS) * ngain
            else:
                nf[at : at + 40, :] = jnp.zeros((40, 128), F32)
        nf[128 * g + 120 : 128 * g + 128, :] = jnp.zeros((8, 128), F32)

    nt = (((1,), (1,)), ((), ()))

    @pl.loop(0, NG)
    def _(g):
        n_g = nf[pl.ds(pl.multiple_of(g * 128, 128), 128), :].astype(BF16)
        p = lax.dot_general(wt[...], n_g, nt, preferred_element_type=F32)
        left = jax.nn.sigmoid(p[0:128]) * p[128:256]
        right = jax.nn.sigmoid(p[256:384]) * p[384:512]
        for t in range(NZ):
            zs[t, g] = jnp.concatenate([left[8 * t : 8 * t + 8], right[8 * t : 8 * t + 8]], axis=0).astype(BF16)

    pl.semaphore_wait(barrier, len(greeted))

    for ci, (g0, m) in enumerate(CHUNKS):
        for d in far_first:
            t, to = along(d)
            remote(zs.at[t, pl.ds(g0, m)], zr.at[z, pl.ds(g0, m)], zss.at[ci], zrs.at[ci], to)

    zr[z] = zs[z]

    @pl.loop(0, NG)
    def _(g):
        rows = pl.ds(pl.multiple_of(g * 128, 128), 128)
        gat[rows, :] = jax.nn.sigmoid(jnp.dot(nf[rows, :].astype(BF16), gatew_ref[...], preferred_element_type=F32))

    gcol[...] = jnp.broadcast_to(ogain_ref[...], (128, 128)).T

    lane = lanes_of((NZ, 128))

    def regroup(src, dst, g):
        for y in range(2):
            for q in range(3):
                parts = [src[(3 * q + s) * 2 + y, g].astype(F32) for s in range(3 if q < 2 else 2)]
                for k in range(3):
                    moved = [pltpu.roll(v, (40 * (s - k)) % 128, 1) if s != k else v for s, v in enumerate(parts)]
                    tile = jnp.where(lane < 40, moved[0], moved[1])
                    if len(moved) > 2:
                        tile = jnp.where(lane < 80, tile, moved[2])
                    dst[pl.ds(pl.multiple_of(((g * 2 + y) * 3 + k) * NZ, NZ), NZ), q * 128 : q * 128 + 128] = tile.astype(BF16)

    tn = (((0,), (0,)), ((), ()))
    l_me, r_me = (x0 * 4 + yh * 2 + core) * 2 + yl, (x1 * 4 + x0 * 2 + core) * 2 + yl

    def plane_in(ci):
        g0, m = CHUNKS[ci]
        for src, dst, sem in ((lb, lt, lrs.at[ci]), (rb, rt_, rrs.at[ci])):
            all_of(src.at[pl.ds(0, 15), pl.ds(g0, m)], sem)

            @pl.loop(g0, g0 + m)
            def _(g, src=src, dst=dst):
                regroup(src, dst, g)
        rows = pl.ds(g0 * 96, m * 96)
        return lax.dot_general(rt_[rows, :], lt[rows, :], tn, preferred_element_type=F32)

    for ci, (g0, m) in enumerate(CHUNKS):
        all_of(zr.at[pl.ds(0, 15), pl.ds(g0, m)], zrs.at[ci])

        @pl.loop(g0, g0 + m)
        def _(g):
            for t in range(NZ):
                tb[16 * t : 16 * t + 16, :] = zr[t, g].astype(F32)
            for c in range(16):
                ps[c, g] = tb[pl.ds(c, NZ, stride=16), :].astype(BF16)

        for f, h in zip(left_partners, right_partners):
            to, c = flipped(f)
            remote(ps.at[c, pl.ds(g0, m)], lb.at[l_me, pl.ds(g0, m)], lss.at[ci], lrs.at[ci], to)
            to, c = flipped(h)
            remote(ps.at[8 + c, pl.ds(g0, m)], rb.at[r_me, pl.ds(g0, m)], rss.at[ci], rrs.at[ci], to)

        lb[l_me, pl.ds(g0, m)] = ps[channel, pl.ds(g0, m)]
        rb[r_me, pl.ds(g0, m)] = ps[8 + channel, pl.ds(g0, m)]
        if ci > 0:
            part = plane_in(ci - 1)
            total[...] = part if ci == 1 else total[...] + part
    s_t = plane_in(NCH - 1)
    if NCH > 1:
        s_t = s_t + total[...]
    for r in range(8):
        at = 128 * (r // 3) + 40 * (r % 3)
        for q in range(3):
            st[q * 320 + r * 40 : q * 320 + r * 40 + 40, :] = s_t[at : at + 40, 128 * q : 128 * q + 128]

    lane8 = lanes_of((8, 128))

    for ci in range(NBC):
        l0, m = BACK[ci]
        for y in range(2):
            for l in range(l0, l0 + m):
                for q in range(3):
                    out = []
                    for h in range(2):
                        parts = [st[pl.ds(q * 320 + 160 * y + 10 * h + 3 * l + k, 8, stride=20), :] for k in range(3 if l < 3 else 1)]
                        per = []
                        for r in range(3 if q < 2 else 2):
                            moved = [pltpu.roll(v, (40 * (k - r)) % 128, 1) if k != r else v for k, v in enumerate(parts)]
                            moved += [jnp.zeros((8, 128), F32)] * (3 - len(moved))
                            per.append(jnp.where(lane8 < 40, moved[0], jnp.where(lane8 < 80, moved[1], moved[2])))
                        out.append(per)
                    for r in range(len(out[0])):
                        tiles[(3 * q + r) * 2 + y, l] = jnp.concatenate([out[0][r], out[1][r]], axis=0).astype(BF16)

        for f in left_partners:
            to, _ = flipped(f)
            owner = l_me + 2 * sum(flips[n][0] for n in f if n != "yl") + (1 - 2 * yl if "yl" in f else 0)
            remote(tiles.at[owner, pl.ds(l0, m)], back.at[channel * 2 + yh, pl.ds(l0, m)], ess.at[ci], ers.at[ci], to)
        back[channel * 2 + yh, pl.ds(l0, m)] = tiles[l_me, pl.ds(l0, m)]

    for ci, (l0, m) in enumerate(BACK):
        all_of(back.at[pl.ds(0, 15), pl.ds(l0, m)], ers.at[ci])

        @pl.loop(l0, l0 + m)
        def _(l):
            for h in range(2):
                for c in range(8):
                    tb[16 * c : 16 * c + 16, :] = back[c * 2 + h, l].astype(F32)
                for k in range(8):
                    rows = [tb[pl.ds(8 * u + k, 8, stride=16), :] for u in range(2)]
                    zb[8 * (k // 4) + 4 * h + k % 4, l] = jnp.concatenate(rows, axis=0).astype(BF16)

        for d in far_first:
            t, to = along(d)
            remote(zb.at[t, pl.ds(l0, m)], zo.at[z, pl.ds(l0, m)], bss.at[ci], brs.at[ci], to)
        zo[z, pl.ds(l0, m)] = zb[z, pl.ds(l0, m)]

    for l in range(NL):
        for ci, (l0, m) in enumerate(BACK):
            if l == l0:
                all_of(zo.at[pl.ds(0, 15), pl.ds(l0, m)], brs.at[ci])
        for h in range(2):
            v = jnp.concatenate([zo[t, l].astype(F32)[8 * h : 8 * h + 8] for t in range(NZ)], axis=0)
            center = jnp.mean(v, axis=0, keepdims=True)
            shifted = v - center
            spread = jnp.mean(shifted * shifted, axis=0, keepdims=True)
            x = (shifted * lax.rsqrt(spread + EPS) * gcol[...]).astype(BF16)
            u = lax.dot_general(x, outw_ref[...], tn, preferred_element_type=F32)
            for k in range(3 if l < 3 else 1):
                j = 10 * h + 3 * l + k
                at = 128 * (j // 3) + 40 * (j % 3)
                out_ref[j] = (pair_ref[j].astype(F32) + gat[at : at + 40, :] * u[40 * k : 40 * k + 40]).astype(BF16)

    for ci, (g0, m) in enumerate(CHUNKS):
        for ref, sem in ((zs, zss), (ps, lss), (ps, rss)):
            all_of(ref.at[pl.ds(0, 15), pl.ds(g0, m)], sem.at[ci])
    for ci, (l0, m) in enumerate(BACK):
        for ref, sem in ((tiles, ess), (zb, bss)):
            all_of(ref.at[pl.ds(0, 15), pl.ds(l0, m)], sem.at[ci])


def shards(pair, norm_gain, proj_weight, gate_weight, out_gain, out_weight):
    vm = pl.BlockSpec(memory_space=pltpu.VMEM)
    dma = pltpu.SemaphoreType.DMA
    out = pl.pallas_call(
        kernel,
        out_shape=jax.ShapeDtypeStruct((COLS, ROWS, 128), BF16),
        in_specs=[pl.BlockSpec(memory_space=pl.ANY)] * 6,
        out_specs=vm,
        scratch_shapes=[
            pltpu.VMEM((COLS, ROWS, 128), BF16),
            pltpu.VMEM((1, 128), F32),
            pltpu.VMEM((128, 512), BF16),
            pltpu.VMEM((128, 128), BF16),
            pltpu.VMEM((1, 128), F32),
            pltpu.VMEM((128, 128), BF16),
            pltpu.VMEM((NG * 128, 128), F32),
            pltpu.VMEM((NG * 128, 128), F32),
            pltpu.VMEM((512, 128), BF16),
            pltpu.VMEM((NZ, NG, 16, 128), BF16),
            pltpu.VMEM((NZ, NG, 16, 128), BF16),
            pltpu.VMEM((256, 128), F32),
            pltpu.VMEM((16, NG, 16, 128), BF16),
            pltpu.VMEM((16, NG, 16, 128), BF16),
            pltpu.VMEM((16, NG, 16, 128), BF16),
            pltpu.VMEM((KROWS, 384), BF16),
            pltpu.VMEM((KROWS, 384), BF16),
            pltpu.VMEM((384, 384), F32),
            pltpu.VMEM((960, 128), F32),
            pltpu.VMEM((16, NL, 16, 128), BF16),
            pltpu.VMEM((16, NL, 16, 128), BF16),
            pltpu.VMEM((NZ, NL, 16, 128), BF16),
            pltpu.VMEM((NZ, NL, 16, 128), BF16),
            pltpu.VMEM((128, 128), F32),
            dma((NCH,)), dma((NCH,)), dma((NCH,)), dma((NCH,)), dma((NCH,)), dma((NCH,)),
            dma((NBC,)), dma((NBC,)), dma((NBC,)), dma((NBC,)), dma((6,)),
        ],
        compiler_params=pltpu.CompilerParams(collective_id=0, has_side_effects=True, vmem_limit_bytes=63 * 1024 * 1024),
        name="triangle",
    )(jnp.transpose(pair, (1, 0, 2)), norm_gain.reshape(1, -1), proj_weight, gate_weight, out_gain.reshape(1, -1), out_weight)
    return jnp.transpose(out, (1, 0, 2))


def solution(mesh):
    in_specs = (P("row", "col", None), P(), P(), P(), P(), P())
    return jax.shard_map(shards, mesh=mesh, in_specs=in_specs, out_specs=P("row", "col", None), check_vma=False)
```

time: 433 us -> 66.5 us (0.15)
  the two profiles are of different devices: /device:TPU:2 before, /device:TPU:1 now
where the time goes in v2:
time: 66.5 us; the launch traced here: 66.1 us
  Pallas kernels  64.5 us (97%)
  local copies, waits for them, and re-layouts  1.63 us (2%)
    pallas_call x1, Pallas kernels, shards(): pl.pallas_call(kernel, out_shape=jax.ShapeDtypeStruct((COLS, ROWS, 128),...  64.5 us
    unnamed x1, local copies, waits for them, and re-layouts  1.63 us

profile of v2, /device:TPU:1, one launch (start us, length us, event | category | flops | bytes accessed | tf_op | source)
XLA Modules:
  0.0 66.1 jit_solution(9875449951179266512)
XLA Ops:
  0.0 64.5 %triangle.1 = bf16[20,40,128]{2,1,0:T(8,128)(2,1)} custom-call(bf16[20,40,128]{2,1,0:T(8,128)(2,1)} %bitcast.5, f32[1,128]{1,0:T(1,128)} %bitcast.6, bf16[128,512]{1,0:T(8,128)(2,1)} %proj_in.1, bf16[128,128]{1,0:T(8,128)(2,1)} %gatew_in.1, f32[1,128]{1,0:T(1,128)} %bitcast.7, bf16[128,128]{1,0:T(8,128)(2,1)} %outw_in.1), custom_call_target="tpu_custom_call" | custom-call | tf_op jit(solution)/shard_map/triangle/pallas_call | solution.py:251
  64.5 1.6 %copy.8 = bf16[40,20,128]{2,0,1:T(8,128)(2,1)} copy(bf16[40,20,128]{2,0,1:T(8,128)(2,1)} %bitcast.4) | data formatting | bytes 409600

commit v3 on v2

--- a/solution.py
+++ b/solution.py
@@ -31,28 +31,32 @@
 
 def kernel(pair_in, ngain_in, proj_in, gatew_in, ogain_in, outw_in, out_ref,
            pair_ref, ngain_ref, proj_ref, gatew_ref, ogain_ref, outw_ref, nf, gat, wt, zs, zr, tb, ps, lb, rb, lt, rt_, total, st, tiles, back, zb, zo, gcol,
-           zss, zrs, lss, lrs, rss, rrs, ess, ers, bss, brs, ins):
+           zss, zrs, lss, lrs, rss, rrs, fss, frs, ess, ers, bss, brs, ins):
     row = lax.axis_index("row")
     col = lax.axis_index("col")
     z, yl = col % NZ, col // NZ
     x1, x0, yh, core = row // 8, (row // 4) % 2, (row // 2) % 2, row % 2
 
-    flips = {"x1": (8 * (1 - 2 * x1), 0, 0), "x0": (4 * (1 - 2 * x0), 0, 4 * (1 - 2 * x0)), "yh": (2 * (1 - 2 * yh), 0, 0),
-             "core": (1 - 2 * core, 0, 1 - 2 * core), "yl": (0, NZ * (1 - 2 * yl), 2 * (1 - 2 * yl))}
-    channel = x0 * 4 + yl * 2 + core
+    fx1, fx0, fyh, fyl = 1 - 2 * x1, 1 - 2 * x0, 1 - 2 * yh, 1 - 2 * yl
+    flips = {"x1": (8 * fx1, 0, 4 * fx1, 8 * fx1), "x0": (4 * fx0, 0, 2 * fx0, 4 * fx0),
+             "yh": (2 * fyh, 0, 0, 2 * fyh), "yl": (0, NZ * fyl, fyl, fyl)}
+    channel = x1 * 4 + x0 * 2 + yl
+    place = (x1 * 4 + x0 * 2 + yh) * 2 + yl
+    r_place = core * 8 + (x1 * 2 + x0) * 2 + yl
+    sibling = {"row": row + 1 - 2 * core, "col": col}
 
     def flipped(names):
-        r, c, k = row, col, channel
+        r, c, k, p = row, col, channel, place
         for name in names:
-            r, c, k = r + flips[name][0], c + flips[name][1], k + flips[name][2]
-        return {"row": r, "col": c}, k
+            r, c, k, p = r + flips[name][0], c + flips[name][1], k + flips[name][2], p + flips[name][3]
+        return {"row": r, "col": c}, k, p
 
     def subsets(names):
-        found = [[n for i, n in enumerate(names) if m >> i & 1] for m in range(1, 16)]
+        found = [[n for i, n in enumerate(names) if m >> i & 1] for m in range(1, 2 ** len(names))]
         return sorted(found, key=lambda f: -len(f))
 
-    left_partners = subsets(("x0", "yh", "yl", "core"))
-    right_partners = subsets(("x1", "x0", "yl", "core"))
+    left_partners = subsets(("x1", "x0", "yh", "yl"))
+    right_partners = subsets(("x1", "x0", "yl"))
     far_first = [8] + [d for k in range(7, 0, -1) for d in (k, NZ - k)]
 
     def along(d):
@@ -74,48 +78,52 @@
 
     barrier = pltpu.get_barrier_semaphore()
     greeted = [along(d)[1] for d in far_first]
-    greeted += [flipped(f)[0] for f in left_partners] + [flipped(f)[0] for f in right_partners if "x1" in f]
+    greeted += [flipped(f)[0] for f in left_partners] + [sibling]
     for to in greeted:
         pl.semaphore_signal(barrier, inc=1, device_id=to, device_id_type=MESH)
 
-    for f in fetch:
-        f.wait()
-    wt[...] = proj_ref[...].astype(F32).T.astype(BF16)
-    ngain = ngain_ref[...]
-
-    for g in range(NG):
-        for s in range(3):
-            at = 128 * g + 40 * s
-            if 3 * g + s < COLS:
-                v = pair_ref[3 * g + s].astype(F32)
-                center = jnp.mean(v, axis=-1, keepdims=True)
-                shifted = v - center
-                spread = jnp.mean(shifted * shifted, axis=-1, keepdims=True)
-                nf[at : at + 40, :] = shifted * lax.rsqrt(spread + EPS) * ngain
-            else:
-                nf[at : at + 40, :] = jnp.zeros((40, 128), F32)
-        nf[128 * g + 120 : 128 * g + 128, :] = jnp.zeros((8, 128), F32)
-
     nt = (((1,), (1,)), ((), ()))
-
-    @pl.loop(0, NG)
-    def _(g):
-        n_g = nf[pl.ds(pl.multiple_of(g * 128, 128), 128), :].astype(BF16)
-        p = lax.dot_general(wt[...], n_g, nt, preferred_element_type=F32)
-        left = jax.nn.sigmoid(p[0:128]) * p[128:256]
-        right = jax.nn.sigmoid(p[256:384]) * p[384:512]
-        for t in range(NZ):
-            zs[t, g] = jnp.concatenate([left[8 * t : 8 * t + 8], right[8 * t : 8 * t + 8]], axis=0).astype(BF16)
-
-    pl.semaphore_wait(barrier, len(greeted))
-
     for ci, (g0, m) in enumerate(CHUNKS):
+        if ci == 0:
+            fetch[0].wait()
+            fetch[2].wait()
+        ngain = ngain_ref[...]
+        for g in range(g0, g0 + m):
+            for s in range(3):
+                at = 128 * g + 40 * s
+                if 3 * g + s < COLS:
+                    v = pair_ref[3 * g + s].astype(F32)
+                    center = jnp.mean(v, axis=-1, keepdims=True)
+                    shifted = v - center
+                    spread = jnp.mean(shifted * shifted, axis=-1, keepdims=True)
+                    nf[at : at + 40, :] = shifted * lax.rsqrt(spread + EPS) * ngain
+                else:
+                    nf[at : at + 40, :] = jnp.zeros((40, 128), F32)
+            nf[128 * g + 120 : 128 * g + 128, :] = jnp.zeros((8, 128), F32)
+        if ci == 0:
+            fetch[1].wait()
+            wt[...] = proj_ref[...].astype(F32).T.astype(BF16)
+
+        @pl.loop(g0, g0 + m)
+        def _(g):
+            n_g = nf[pl.ds(pl.multiple_of(g * 128, 128), 128), :].astype(BF16)
+            p = lax.dot_general(wt[...], n_g, nt, preferred_element_type=F32)
+            left = jax.nn.sigmoid(p[0:128]) * p[128:256]
+            right = jax.nn.sigmoid(p[256:384]) * p[384:512]
+            for t in range(NZ):
+                zs[t, g] = jnp.concatenate([left[8 * t : 8 * t + 8], right[8 * t : 8 * t + 8]], axis=0).astype(BF16)
+
+        if ci == 0:
+            pl.semaphore_wait(barrier, len(greeted))
+
         for d in far_first:
             t, to = along(d)
             remote(zs.at[t, pl.ds(g0, m)], zr.at[z, pl.ds(g0, m)], zss.at[ci], zrs.at[ci], to)
 
     zr[z] = zs[z]
 
+    for n in (3, 4, 5):
+        fetch[n].wait()
     @pl.loop(0, NG)
     def _(g):
         rows = pl.ds(pl.multiple_of(g * 128, 128), 128)
@@ -125,10 +133,10 @@
 
     lane = lanes_of((NZ, 128))
 
-    def regroup(src, dst, g):
+    def regroup(src, dst, g, at):
         for y in range(2):
             for q in range(3):
-                parts = [src[(3 * q + s) * 2 + y, g].astype(F32) for s in range(3 if q < 2 else 2)]
+                parts = [src[at(3 * q + s) + y, g].astype(F32) for s in range(3 if q < 2 else 2)]
                 for k in range(3):
                     moved = [pltpu.roll(v, (40 * (s - k)) % 128, 1) if s != k else v for s, v in enumerate(parts)]
                     tile = jnp.where(lane < 40, moved[0], moved[1])
@@ -137,16 +145,24 @@
                     dst[pl.ds(pl.multiple_of(((g * 2 + y) * 3 + k) * NZ, NZ), NZ), q * 128 : q * 128 + 128] = tile.astype(BF16)
 
     tn = (((0,), (0,)), ((), ()))
-    l_me, r_me = (x0 * 4 + yh * 2 + core) * 2 + yl, (x1 * 4 + x0 * 2 + core) * 2 + yl
 
     def plane_in(ci):
         g0, m = CHUNKS[ci]
-        for src, dst, sem in ((lb, lt, lrs.at[ci]), (rb, rt_, rrs.at[ci])):
-            all_of(src.at[pl.ds(0, 15), pl.ds(g0, m)], sem)
-
-            @pl.loop(g0, g0 + m)
-            def _(g, src=src, dst=dst):
-                regroup(src, dst, g)
+        all_of(rb.at[pl.ds(0, 7), pl.ds(g0, m)], rrs.at[ci])
+        mine = rb.at[pl.ds(8 * core, 8), pl.ds(g0, m)]
+        remote(mine, mine, fss.at[ci], frs.at[ci], sibling)
+        all_of(lb.at[pl.ds(0, 15), pl.ds(g0, m)], lrs.at[ci])
+
+        @pl.loop(g0, g0 + m)
+        def _(g):
+            regroup(lb, lt, g, lambda i: 2 * i)
+
+        all_of(rb.at[pl.ds(0, 8), pl.ds(g0, m)], frs.at[ci])
+
+        @pl.loop(g0, g0 + m)
+        def _(g):
+            regroup(rb, rt_, g, lambda j: 8 * (j % 2) + 2 * (j // 2))
+
         rows = pl.ds(g0 * 96, m * 96)
         return lax.dot_general(rt_[rows, :], lt[rows, :], tn, preferred_element_type=F32)
 
@@ -160,14 +176,15 @@
             for c in range(16):
                 ps[c, g] = tb[pl.ds(c, NZ, stride=16), :].astype(BF16)
 
-        for f, h in zip(left_partners, right_partners):
-            to, c = flipped(f)
-            remote(ps.at[c, pl.ds(g0, m)], lb.at[l_me, pl.ds(g0, m)], lss.at[ci], lrs.at[ci], to)
-            to, c = flipped(h)
-            remote(ps.at[8 + c, pl.ds(g0, m)], rb.at[r_me, pl.ds(g0, m)], rss.at[ci], rrs.at[ci], to)
-
-        lb[l_me, pl.ds(g0, m)] = ps[channel, pl.ds(g0, m)]
-        rb[r_me, pl.ds(g0, m)] = ps[8 + channel, pl.ds(g0, m)]
+        rb[r_place, pl.ds(g0, m)] = ps[8 + channel, pl.ds(g0, m)]
+        lb[place, pl.ds(g0, m)] = ps[channel, pl.ds(g0, m)]
+        for f in right_partners:
+            to, c, _ = flipped(f)
+            remote(ps.at[8 + c, pl.ds(g0, m)], rb.at[r_place, pl.ds(g0, m)], rss.at[ci], rrs.at[ci], to)
+        for f in left_partners:
+            to, c, _ = flipped(f)
+            remote(ps.at[c, pl.ds(g0, m)], lb.at[place, pl.ds(g0, m)], lss.at[ci], lrs.at[ci], to)
+
         if ci > 0:
             part = plane_in(ci - 1)
             total[...] = part if ci == 1 else total[...] + part
@@ -199,10 +216,9 @@
                         tiles[(3 * q + r) * 2 + y, l] = jnp.concatenate([out[0][r], out[1][r]], axis=0).astype(BF16)
 
         for f in left_partners:
-            to, _ = flipped(f)
-            owner = l_me + 2 * sum(flips[n][0] for n in f if n != "yl") + (1 - 2 * yl if "yl" in f else 0)
-            remote(tiles.at[owner, pl.ds(l0, m)], back.at[channel * 2 + yh, pl.ds(l0, m)], ess.at[ci], ers.at[ci], to)
-        back[channel * 2 + yh, pl.ds(l0, m)] = tiles[l_me, pl.ds(l0, m)]
+            to, _, p = flipped(f)
+            remote(tiles.at[p, pl.ds(l0, m)], back.at[channel * 2 + yh, pl.ds(l0, m)], ess.at[ci], ers.at[ci], to)
+        back[channel * 2 + yh, pl.ds(l0, m)] = tiles[place, pl.ds(l0, m)]
 
     for ci, (l0, m) in enumerate(BACK):
         all_of(back.at[pl.ds(0, 15), pl.ds(l0, m)], ers.at[ci])
@@ -238,8 +254,8 @@
                 out_ref[j] = (pair_ref[j].astype(F32) + gat[at : at + 40, :] * u[40 * k : 40 * k + 40]).astype(BF16)
 
     for ci, (g0, m) in enumerate(CHUNKS):
-        for ref, sem in ((zs, zss), (ps, lss), (ps, rss)):
-            all_of(ref.at[pl.ds(0, 15), pl.ds(g0, m)], sem.at[ci])
+        for ref, n, sem in ((zs, 15, zss), (ps, 15, lss), (ps, 7, rss), (rb, 8, fss)):
+            all_of(ref.at[pl.ds(0, n), pl.ds(g0, m)], sem.at[ci])
     for ci, (l0, m) in enumerate(BACK):
         for ref, sem in ((tiles, ess), (zb, bss)):
             all_of(ref.at[pl.ds(0, 15), pl.ds(l0, m)], sem.at[ci])
@@ -278,7 +294,7 @@
             pltpu.VMEM((NZ, NL, 16, 128), BF16),
             pltpu.VMEM((NZ, NL, 16, 128), BF16),
             pltpu.VMEM((128, 128), F32),
-            dma((NCH,)), dma((NCH,)), dma((NCH,)), dma((NCH,)), dma((NCH,)), dma((NCH,)),
+            dma((NCH,)), dma((NCH,)), dma((NCH,)), dma((NCH,)), dma((NCH,)), dma((NCH,)), dma((NCH,)), dma((NCH,)),
             dma((NBC,)), dma((NBC,)), dma((NBC,)), dma((NBC,)), dma((6,)),
         ],
         compiler_params=pltpu.CompilerParams(collective_id=0, has_side_effects=True, vmem_limit_bytes=63 * 1024 * 1024),

time: 66.5 us -> 66.5 us (level)
  no operation moved by 1% of the time
where the time goes in v3:
time: 66.5 us; the launch traced here: 66.3 us
  Pallas kernels  64.7 us (97%)
  local copies, waits for them, and re-layouts  1.63 us (2%)
    pallas_call x1, Pallas kernels, shards(): pl.pallas_call(kernel, out_shape=jax.ShapeDtypeStruct((COLS, ROWS, 128),...  64.7 us
    unnamed x1, local copies, waits for them, and re-layouts  1.63 us

profile of v3, /device:TPU:1, one launch (start us, length us, event | category | flops | bytes accessed | tf_op | source)
XLA Modules:
  0.0 66.3 jit_solution(8218356635354708138)
XLA Ops:
  0.0 64.7 %triangle.1 = bf16[20,40,128]{2,1,0:T(8,128)(2,1)} custom-call(bf16[20,40,128]{2,1,0:T(8,128)(2,1)} %bitcast.5, f32[1,128]{1,0:T(1,128)} %bitcast.6, bf16[128,512]{1,0:T(8,128)(2,1)} %proj_in.1, bf16[128,128]{1,0:T(8,128)(2,1)} %gatew_in.1, f32[1,128]{1,0:T(1,128)} %bitcast.7, bf16[128,128]{1,0:T(8,128)(2,1)} %outw_in.1), custom_call_target="tpu_custom_call" | custom-call | tf_op jit(solution)/shard_map/triangle/pallas_call | solution.py:267
  64.7 1.6 %copy.8 = bf16[40,20,128]{2,0,1:T(8,128)(2,1)} copy(bf16[40,20,128]{2,0,1:T(8,128)(2,1)} %bitcast.4) | data formatting | bytes 409600

commit v4 on v3

--- a/solution.py
+++ b/solution.py
@@ -29,9 +29,9 @@
     return lax.broadcasted_iota(jnp.int32, shape, 0)
 
 
-def kernel(pair_in, ngain_in, proj_in, gatew_in, ogain_in, outw_in, out_ref,
-           pair_ref, ngain_ref, proj_ref, gatew_ref, ogain_ref, outw_ref, nf, gat, wt, zs, zr, tb, ps, lb, rb, lt, rt_, total, st, tiles, back, zb, zo, gcol,
-           zss, zrs, lss, lrs, rss, rrs, fss, frs, ess, ers, bss, brs, ins):
+def kernel(pair_in, ngain_in, proj_in, gatew_in, ogain_in, outw_in, out_hbm,
+           pair_ref, ngain_ref, proj_ref, gatew_ref, ogain_ref, outw_ref, out_ref, nf, gat, wt, zs, zr, tb, ps, lb, rb, lt, rt_, total, st, tiles, back, zb, zo, gcol,
+           zss, zrs, lss, lrs, rss, rrs, fss, frs, ess, ers, bss, brs, ins, outs):
     row = lax.axis_index("row")
     col = lax.axis_index("col")
     z, yl = col % NZ, col // NZ
@@ -237,6 +237,7 @@
             remote(zb.at[t, pl.ds(l0, m)], zo.at[z, pl.ds(l0, m)], bss.at[ci], brs.at[ci], to)
         zo[z, pl.ds(l0, m)] = zb[z, pl.ds(l0, m)]
 
+    leaving = []
     for l in range(NL):
         for ci, (l0, m) in enumerate(BACK):
             if l == l0:
@@ -253,22 +254,27 @@
                 at = 128 * (j // 3) + 40 * (j % 3)
                 out_ref[j] = (pair_ref[j].astype(F32) + gat[at : at + 40, :] * u[40 * k : 40 * k + 40]).astype(BF16)
 
+            j0, n = 10 * h + 3 * l, 3 if l < 3 else 1
+            leaving.append(pltpu.make_async_copy(out_ref.at[pl.ds(j0, n)], out_hbm.at[pl.ds(j0, n)], outs.at[2 * l + h]))
+            leaving[-1].start()
+
     for ci, (g0, m) in enumerate(CHUNKS):
         for ref, n, sem in ((zs, 15, zss), (ps, 15, lss), (ps, 7, rss), (rb, 8, fss)):
             all_of(ref.at[pl.ds(0, n), pl.ds(g0, m)], sem.at[ci])
     for ci, (l0, m) in enumerate(BACK):
         for ref, sem in ((tiles, ess), (zb, bss)):
             all_of(ref.at[pl.ds(0, 15), pl.ds(l0, m)], sem.at[ci])
+    for part in leaving:
+        part.wait()
 
 
 def shards(pair, norm_gain, proj_weight, gate_weight, out_gain, out_weight):
-    vm = pl.BlockSpec(memory_space=pltpu.VMEM)
     dma = pltpu.SemaphoreType.DMA
     out = pl.pallas_call(
         kernel,
         out_shape=jax.ShapeDtypeStruct((COLS, ROWS, 128), BF16),
         in_specs=[pl.BlockSpec(memory_space=pl.ANY)] * 6,
-        out_specs=vm,
+        out_specs=pl.BlockSpec(memory_space=pl.ANY),
         scratch_shapes=[
             pltpu.VMEM((COLS, ROWS, 128), BF16),
             pltpu.VMEM((1, 128), F32),
@@ -276,6 +282,7 @@
             pltpu.VMEM((128, 128), BF16),
             pltpu.VMEM((1, 128), F32),
             pltpu.VMEM((128, 128), BF16),
+            pltpu.VMEM((COLS, ROWS, 128), BF16),
             pltpu.VMEM((NG * 128, 128), F32),
             pltpu.VMEM((NG * 128, 128), F32),
             pltpu.VMEM((512, 128), BF16),
@@ -295,7 +302,7 @@
             pltpu.VMEM((NZ, NL, 16, 128), BF16),
             pltpu.VMEM((128, 128), F32),
             dma((NCH,)), dma((NCH,)), dma((NCH,)), dma((NCH,)), dma((NCH,)), dma((NCH,)), dma((NCH,)), dma((NCH,)),
-            dma((NBC,)), dma((NBC,)), dma((NBC,)), dma((NBC,)), dma((6,)),
+            dma((NBC,)), dma((NBC,)), dma((NBC,)), dma((NBC,)), dma((6,)), dma((2 * NL,)),
         ],
         compiler_params=pltpu.CompilerParams(collective_id=0, has_side_effects=True, vmem_limit_bytes=63 * 1024 * 1024),
         name="triangle",

time: 66.5 us -> 66.5 us (level)
  no operation moved by 1% of the time
where the time goes in v4:
time: 66.5 us; the launch traced here: 66.3 us
  Pallas kernels  64.7 us (97%)
  local copies, waits for them, and re-layouts  1.63 us (2%)
    pallas_call x1, Pallas kernels, shards(): pl.pallas_call(kernel, out_shape=jax.ShapeDtypeStruct((COLS, ROWS, 128),...  64.7 us
    unnamed x1, local copies, waits for them, and re-layouts  1.63 us

profile of v4, /device:TPU:1, one launch (start us, length us, event | category | flops | bytes accessed | tf_op | source)
XLA Modules:
  0.0 66.3 jit_solution(5031144660527292813)
XLA Ops:
  0.0 64.7 %triangle.1 = bf16[20,40,128]{2,1,0:T(8,128)(2,1)} custom-call(bf16[20,40,128]{2,1,0:T(8,128)(2,1)} %bitcast.5, f32[1,128]{1,0:T(1,128)} %bitcast.6, bf16[128,512]{1,0:T(8,128)(2,1)} %proj_in.1, bf16[128,128]{1,0:T(8,128)(2,1)} %gatew_in.1, f32[1,128]{1,0:T(1,128)} %bitcast.7, bf16[128,128]{1,0:T(8,128)(2,1)} %outw_in.1), custom_call_target="tpu_custom_call" | custom-call | tf_op jit(solution)/shard_map/triangle/pallas_call | solution.py:273
  64.7 1.6 %copy.8 = bf16[40,20,128]{2,0,1:T(8,128)(2,1)} copy(bf16[40,20,128]{2,0,1:T(8,128)(2,1)} %bitcast.4) | data formatting | bytes 409600
